TPU v7x, 256 devices: a whole 4x4x8 slice. The times are simulated.
256 devices in a mesh: tm: 8 (over y, core), space: 32 (over z, x).
Axes of the slice: x: 4, y: 4, z: 8, core: 2. Of those that a mesh axis runs over, the one named last changes fastest.
Arguments:
- feats: bfloat16 [32, 64, 80, 384], P('tm', 'space'), may hold values from -6 to 6
- clip_lengths: int32 [3], replicated, may hold values from 1 to 16, as said below
- norm_gain: float32 [384], replicated, may hold values from 0.1 to 1.9
- conv_weight: bfloat16 [3, 3, 3, 384, 384], replicated, may hold values from -0.109375 to 0.109375
- conv_bias: float32 [384], replicated, may hold values from -3 to 3
- attn_gain: float32 [384], replicated, may hold values from 0.1 to 1.9
- query_weight: bfloat16 [384, 384], replicated, may hold values from -4 to 4
- key_weight: bfloat16 [384, 384], replicated, may hold values from -4 to 4
- value_weight: bfloat16 [384, 384], replicated, may hold values from -0.3125 to 0.3125
- output_weight: bfloat16 [384, 384], replicated, may hold values from -0.3125 to 0.3125
Outputs:
- resid: bfloat16 [32, 64, 80, 384], P('tm', 'space')
- mixed: bfloat16 [32, 64, 80, 384], P('tm', 'space')
Inputs may be any that keep to these rules, and one draw needn't show every extreme that they name: `clip_lengths`: the lengths sum to 32; exactly one clip has 16 frames.
All inputs are finite; a program needn't handle non-finite values.
Results may differ from a plain program's by a relative error of at most 0.0085.
Values may be sent and summed in bfloat16 or wider, within the bound.
A program may use at most 128 MiB of HBM per device.

v0:
```python
import math

import jax
import jax.numpy as jnp
from jax import lax
from jax.sharding import PartitionSpec as P


def padded_2(value, sides, width):
    for axis, dim in sides:
        peers, length = (lax.axis_size(axis), value.shape[dim])
        up = [(i, (i + 1) % peers) for i in range(peers - 1)]
        down = [(j, i) for i, j in up]
        last = lax.slice_in_dim(value, length - width, length, axis=dim)
        first = lax.slice_in_dim(value, 0, width, axis=dim)
        before = lax.ppermute(last, axis, up)
        after = lax.ppermute(first, axis, down)
        value = jnp.concatenate([before, value, after], axis=dim)
    return value


def passed_along(value, axis, by):
    peers = lax.axis_size(axis)
    pairs = [(i, i + by) for i in range(peers) if 0 <= i + by < peers]
    return lax.ppermute(value, axis, pairs)


def normalize(values, scale_gain):
    widened = values.astype(jnp.float32)
    return (
        widened
        * lax.rsqrt(jnp.mean(widened * widened, axis=-1, keepdims=True) + 1e-06)
        * scale_gain
    )


def attend(state_in, queries, keys_in, values_in):
    running_max, running_sum, running_acc = state_in
    scores = jnp.einsum(
        "fqc,fkc->fqk", queries, keys_in, preferred_element_type=jnp.float32
    ) / math.sqrt(queries.shape[-1])
    new_max = jnp.max(scores, axis=-1)
    rescale = jnp.exp(running_max - new_max)
    expanded = jnp.exp(scores - new_max[..., None])
    new_sum = running_sum * rescale + jnp.sum(expanded, axis=-1)
    new_acc = running_acc * rescale[..., None] + jnp.einsum(
        "fqk,fkc->fqc", expanded.astype(jnp.bfloat16), values_in, preferred_element_type=jnp.float32
    )
    return (new_max, new_sum, new_acc)


def local(
    feats,
    clip_lengths,
    norm_gain,
    conv_weight,
    conv_bias,
    attn_gain,
    query_weight,
    key_weight,
    value_weight,
    output_weight,
):
    frame_count, row_count, col_count, channels = feats.shape
    pixel_count = row_count * col_count
    active = jax.nn.silu(normalize(feats, norm_gain)).astype(jnp.bfloat16)
    rimmed = padded_2(active, (("space", 1),), 1)
    last_frames = rimmed[frame_count - 2 :]
    nearer = passed_along(last_frames, "tm", 1)
    extended = jnp.concatenate([nearer, rimmed], axis=0)
    padded = jnp.pad(extended, ((0, 0), (0, 0), (1, 1), (0, 0)))
    global_frame = lax.axis_index("tm") * frame_count + jnp.arange(frame_count, dtype=jnp.int32)
    clip_ends = jnp.cumsum(clip_lengths)
    clip_starts = jnp.sum(
        clip_lengths[None, :] * (clip_ends[None, :] <= global_frame[:, None]).astype(jnp.int32),
        axis=1,
    )
    conv_sum = jnp.zeros((frame_count * pixel_count, channels), jnp.float32)
    for time_lag in range(3):
        live_mask = (global_frame - time_lag >= clip_starts).astype(jnp.bfloat16)[
            :, None, None, None
        ]
        for row_offset in range(3):
            for col_offset in range(3):
                window = (
                    padded[
                        2 - time_lag : 2 - time_lag + frame_count,
                        row_offset : row_offset + row_count,
                        col_offset : col_offset + col_count,
                    ]
                    * live_mask
                )
                conv_sum = conv_sum + jnp.dot(
                    window.reshape(-1, channels),
                    conv_weight[time_lag, row_offset, col_offset],
                    preferred_element_type=jnp.float32,
                )
    resid_flat = (feats.astype(jnp.float32).reshape(-1, channels) + conv_sum + conv_bias).astype(
        jnp.bfloat16
    )
    normed = normalize(resid_flat, attn_gain).astype(jnp.bfloat16)
    queries = (
        jnp.dot(normed, query_weight, preferred_element_type=jnp.float32)
        .astype(jnp.bfloat16)
        .reshape(frame_count, pixel_count, channels)
    )
    initial = (
        jnp.full((frame_count, pixel_count), -jnp.inf, jnp.float32),
        jnp.zeros((frame_count, pixel_count), jnp.float32),
        jnp.zeros((frame_count, pixel_count, channels), jnp.float32),
    )
    keys_local = (
        jnp.dot(normed, key_weight, preferred_element_type=jnp.float32)
        .astype(jnp.bfloat16)
        .reshape(frame_count, pixel_count, channels)
    )
    values_local = (
        jnp.dot(normed, value_weight, preferred_element_type=jnp.float32)
        .astype(jnp.bfloat16)
        .reshape(frame_count, pixel_count, channels)
    )
    state_out = attend(
        initial,
        queries,
        lax.all_gather(keys_local, "space", axis=1, tiled=True),
        lax.all_gather(values_local, "space", axis=1, tiled=True),
    )
    attended = (state_out[2] / state_out[1][..., None]).astype(jnp.bfloat16).reshape(-1, channels)
    mixed = (
        resid_flat.astype(jnp.float32)
        + jnp.dot(attended, output_weight, preferred_element_type=jnp.float32)
    ).astype(jnp.bfloat16)
    return (
        resid_flat.reshape(frame_count, row_count, col_count, channels),
        mixed.reshape(frame_count, row_count, col_count, channels),
    )


def solution(mesh):
    return jax.shard_map(
        local,
        mesh=mesh,
        in_specs=(P("tm", "space", None, None), P(), P(), P(), P(), P(), P(), P(), P(), P()),
        out_specs=(P("tm", "space", None, None), P("tm", "space", None, None)),
        check_vma=False,
    )
```

profile of v0, /device:TPU:41, one launch (start us, length us, event | category | flops | bytes accessed | tf_op | source)
XLA Modules:
  0.0 347.4 jit_solution(10180359243093162032)
XLA Ops:
  7.2 0.9 reduce-window.8
  8.1 0.8 select_reduce_fusion
  8.9 1.3 multiply_reduce_fusion.1
  10.2 1.5 broadcast_multiply_fusion
  11.7 3.1 collective-permute-start
  14.9 4.3 %collective-permute-start.1 = (bf16[4,1,80,384]{3,2,1,0:T(8,128)(2,1)S(1)}, bf16[4,1,80,384]{3,2,1,0:T(8,128)(2,1)S(1)}, u32[]{:S(2)}, u32[]{:S(2)}) collective-permute-start(bf16[4,1,80,384]{3,2,1,0:T(8,128)(2,1)S(1)} %get-tuple-element.31), channel_id=1, source_target_pairs={{1,0},{2,1},{3,2},{4,3},{5,4},{6,5},{7,6},{8,7},{9,8},{10,9},{11,1... | collective-permute-start | bytes 737288 | tf_op jit(solution)/shard_map/ppermute | solution.py:17
  19.1 3.4 collective-permute-done
  22.6 0.9 collective-permute-done.1
  23.5 5.0 %collective-permute-start.2 = (bf16[2,4,80,384]{3,2,1,0:T(8,128)(2,1)S(1)}, bf16[2,4,80,384]{3,2,1,0:T(8,128)(2,1)S(1)}, u32[]{:S(2)}, u32[]{:S(2)}) collective-permute-start(bf16[2,4,80,384]{3,2,1,0:T(8,128)(2,1)S(1)} %pad_maximum_fusion.2), channel_id=1, source_target_pairs={{0,32},{32,64},{64,96},{96,128},{128,160},{160,192},{192,224},{1,3... | collective-permute-start | bytes 1474568 | tf_op jit(solution)/shard_map/ppermute | solution.py:25
  28.5 5.8 %collective-permute-done.2 = bf16[2,4,80,384]{3,2,1,0:T(8,128)(2,1)S(1)} collective-permute-done((bf16[2,4,80,384]{3,2,1,0:T(8,128)(2,1)S(1)}, bf16[2,4,80,384]{3,2,1,0:T(8,128)(2,1)S(1)}, u32[]{:S(2)}, u32[]{:S(2)}) %collective-permute-start.2) | collective-permute-done | bytes 491552 | tf_op jit(solution)/shard_map/ppermute | solution.py:25
  34.5 1.1 slice_multiply_fusion.12
  35.6 1.1 slice_multiply_fusion.6
  36.7 1.0 slice_multiply_fusion.18
  38.5 0.5 convolution_add_fusion.25
  38.9 0.5 convolution_add_fusion.24
  39.9 0.5 convolution_add_fusion.22
  40.3 0.5 convolution_add_fusion.21
  41.3 0.5 convolution_add_fusion.19
  41.7 0.5 convolution_add_fusion.18
  42.2 0.5 convolution_add_fusion.17
  42.7 0.5 convolution_add_fusion.16
  48.2 0.6 convolution_add_fusion.4
  50.3 0.6 fusion.19
  50.9 1.3 convolution_convert_fusion.1
  52.3 1.3 convolution_convert_fusion
  53.7 0.5 convolution_convert_fusion.2
  54.2 136.3 %all-gather.3.cloned.1.call-done = bf16[4,5120,384]{2,1,0:T(8,128)(2,1)} async-done(((bf16[4,160,384]{2,1,0:T(8,128)(2,1)}), bf16[4,5120,384]{2,1,0:T(8,128)(2,1)}) %all-gather.3.cloned.1.call-update) | async-done | bytes 15728656 | tf_op jit(solution)/shard_map/all_gather | solution.py:125
  190.6 15.6 %multiply_reduce_fusion = (f32[4,160]{1,0:T(4,128)S(1)}, f32[4,160,5120]{2,1,0:T(8,128)}) fusion(bf16[4,160,384]{2,1,0:T(8,128)(2,1)S(1)} %bitcast.186, bf16[4,5120,384]{2,1,0:T(8,128)(2,1)} %all-gather.3.cloned.1.call-done), kind=kOutput, calls=%fused_computation.1 | convolution fusion | flops 2523135488 | bytes 29329920 | tf_op jit(solution)/shard_map/fqc,fkc->fqk/dot_general | solution.py:39
  206.1 7.2 %fusion = f32[4,160]{1,0:T(4,128)S(1)} fusion(f32[4,160,5120]{2,1,0:T(8,128)} %get-tuple-element.42, f32[4,160]{1,0:T(4,128)S(1)} %get-tuple-element.41), kind=kLoop, calls=%fused_computation.2 | loop fusion | flops 9829760 | bytes 13112320 | tf_op jit(solution)/shard_map/reduce_sum | solution.py:45
  213.3 112.8 %all-gather.5.cloned.1.call-done = bf16[4,5120,384]{2,1,0:T(8,128)(2,1)} async-done(((bf16[4,160,384]{2,1,0:T(8,128)(2,1)}), bf16[4,5120,384]{2,1,0:T(8,128)(2,1)}) %all-gather.5.cloned.1.call-update) | async-done | bytes 15728656 | tf_op jit(solution)/shard_map/all_gather | solution.py:126
  326.1 13.2 %fusion.16 = bf16[4,160,384]{2,1,0:T(8,128)(2,1)S(1)} fusion(bf16[4,5120,384]{2,1,0:T(8,128)(2,1)} %all-gather.5.cloned.1.call-done, f32[4,160,5120]{2,1,0:T(8,128)} %get-tuple-element.42, f32[4,160]{1,0:T(4,128)S(1)} %get-tuple-element.41, f32[4,160]{1,0:T(4,128)S(1)} %get-tuple-element.33, f32[4,160]{1,0:T(4,128)S(1)} %get-tuple-element.32), kind=kOutput, calls=%fused_computation.46 | convolution fusion | flops 2527150080 | bytes 29335040 | tf_op jit(solution)/shard_map/fqk,fkc->fqc/dot_general | solution.py:46
  339.3 1.2 fusion.8
  (52 shorter events, 8.5 us)
Async XLA Ops:
  7.2 43.8 %copy-start = (bf16[384,384]{1,0:T(8,128)(2,1)S(1)}, bf16[384,384]{1,0:T(8,128)(2,1)}, u32[]{:S(2)}) copy-start(bf16[384,384]{1,0:T(8,128)(2,1)} %param.17) | copy-start | bytes 884740
  7.2 183.4 %all-gather.3.cloned.1.call-start = ((), (), s32[]{:S(2)}) async-start(), calls=%async_computation | async-start | bytes 16220160 | tf_op jit(solution)/shard_map/all_gather | solution.py:125
  11.7 10.8 %collective-permute-start = (bf16[4,1,80,384]{3,2,1,0:T(8,128)(2,1)S(1)}, bf16[4,1,80,384]{3,2,1,0:T(8,128)(2,1)S(1)}, u32[]{:S(2)}, u32[]{:S(2)}) collective-permute-start(bf16[4,1,80,384]{3,2,1,0:T(8,128)(2,1)S(1)} %get-tuple-element.30), channel_id=1, source_target_pairs={{0,1},{1,2},{2,3},{3,4},{4,5},{5,6},{6,7},{7,8},{8,9},{9,10},{10,1... | collective-permute-start | bytes 737288 | tf_op jit(solution)/shard_map/ppermute | solution.py:16
  14.9 8.6 %collective-permute-start.1 = (bf16[4,1,80,384]{3,2,1,0:T(8,128)(2,1)S(1)}, bf16[4,1,80,384]{3,2,1,0:T(8,128)(2,1)S(1)}, u32[]{:S(2)}, u32[]{:S(2)}) collective-permute-start(bf16[4,1,80,384]{3,2,1,0:T(8,128)(2,1)S(1)} %get-tuple-element.31), channel_id=1, source_target_pairs={{1,0},{2,1},{3,2},{4,3},{5,4},{6,5},{7,6},{8,7},{9,8},{10,9},{11,1... | collective-permute-start | bytes 737288 | tf_op jit(solution)/shard_map/ppermute | solution.py:17
  23.5 10.7 %collective-permute-start.2 = (bf16[2,4,80,384]{3,2,1,0:T(8,128)(2,1)S(1)}, bf16[2,4,80,384]{3,2,1,0:T(8,128)(2,1)S(1)}, u32[]{:S(2)}, u32[]{:S(2)}) collective-permute-start(bf16[2,4,80,384]{3,2,1,0:T(8,128)(2,1)S(1)} %pad_maximum_fusion.2), channel_id=1, source_target_pairs={{0,32},{32,64},{64,96},{96,128},{128,160},{160,192},{192,224},{1,3... | collective-permute-start | bytes 1474568 | tf_op jit(solution)/shard_map/ppermute | solution.py:25
  34.5 3.3 slice-start
  35.6 2.4 slice-start.1
  47.3 3.0 copy-start.2
  47.3 3.0 copy-start.5
  47.7 3.2 copy-start.8
  48.2 4.1 %copy-start.6 = (bf16[384,384]{1,0:T(8,128)(2,1)S(1)}, bf16[384,384]{1,0:T(8,128)(2,1)}, u32[]{:S(2)}) copy-start(bf16[384,384]{1,0:T(8,128)(2,1)} %param.18) | copy-start | bytes 884740
  48.9 4.8 %copy-start.7 = (bf16[384,384]{1,0:T(8,128)(2,1)S(1)}, bf16[384,384]{1,0:T(8,128)(2,1)}, u32[]{:S(2)}) copy-start(bf16[384,384]{1,0:T(8,128)(2,1)} %param.16) | copy-start | bytes 884740
  50.9 288.4 %copy-start.3 = (bf16[640,384]{1,0:T(8,128)(2,1)}, bf16[640,384]{1,0:T(8,128)(2,1)S(1)}, u32[]{:S(2)}) copy-start(bf16[640,384]{1,0:T(8,128)(2,1)S(1)} %get-tuple-element.40) | copy-start | bytes 1474564
  52.3 273.8 %all-gather.5.cloned.1.call-start = ((), (), s32[]{:S(2)}) async-start(), calls=%async_computation.1 | async-start | bytes 16220160 | tf_op jit(solution)/shard_map/all_gather | solution.py:126
  326.1 13.2 %copy-start.4 = (bf16[384,384]{1,0:T(8,128)(2,1)S(1)}, bf16[384,384]{1,0:T(8,128)(2,1)}, u32[]{:S(2)}) copy-start(bf16[384,384]{1,0:T(8,128)(2,1)} %param.19) | copy-start | bytes 884740
  326.1 14.4 %copy-start.1 = (bf16[384,384]{1,0:T(8,128)(2,1)S(1)}, bf16[384,384]{1,0:T(8,128)(2,1)}, u32[]{:S(2)}) copy-start(bf16[384,384]{1,0:T(8,128)(2,1)} %param.17) | copy-start | bytes 884740
Sparse Core Ops, SparseCore 0:
  52.4 138.1 all-gather.2
  193.7 132.3 all-gather.4
where the time goes:
time: 351 us; the launch traced here: 347 us
  waiting for transfers between devices  259 us (74%)
  matrix products  45.7 us (13%)
  other arithmetic  15.2 us (4%)
  between operations  14.5 us (4%)
  starting transfers between devices  12.4 us (4%)
    all_gather x1, waiting for transfers between devices, local(): lax.all_gather(keys_local, 'space', axis=1, tiled=True)  136 us
    all_gather x1, waiting for transfers between devices, local(): lax.all_gather(values_local, 'space', axis=1, tiled=True)  113 us
    dot_general x1, matrix products, attend(): jnp.einsum('fqc,fkc->fqk', queries, keys_in, preferred_element_type=jnp.f...  15.6 us
    dot_general x1, matrix products, attend(): jnp.einsum('fqk,fkc->fqc', expanded.astype(jnp.bfloat16), values_in, pref...  13.2 us
    dot_general x27, matrix products, local(): jnp.dot(window.reshape(-1, channels), conv_weight[time_lag, row_offset, c...  12.6 us
    reduce_sum x1, other arithmetic, attend(): new_sum = running_sum * rescale + jnp.sum(expanded, axis=-1)  7.16 us
  transfers between devices with their start and end apart: 5, of which 5 were waited for; matrix products, arithmetic and copies ran while one was open for 7% of the time, Pallas kernels for 0%

commit v1 on v0

v1 whole, which is shorter than its diff:
```python
import math

import jax
import jax.numpy as jnp
from jax import lax
from jax.experimental import pallas as pl
from jax.experimental.pallas import tpu as pltpu
from jax.sharding import PartitionSpec as P

MESH = pl.DeviceIdType.MESH
COLS = 80
BLK = 2 * COLS
NB = 4
ROWS = NB * BLK
TILE = 320


def scaled(wide, gain):
    mean = jnp.mean(wide * wide, axis=-1, keepdims=True)
    return wide * lax.rsqrt(mean + 1e-06) * gain


def block_kernel(
    feats_ref, clip_ref, norm_gain_ref, conv_hbm, bias_ref, gain_ref, wq_ref, wk_ref, wv_ref, wo_ref,
    resid_ref, out_ref,
    weight, active, taps, conv, rin, kv, qs, acc, top, total, stage,
    w_sem, h_send, h_recv, a_send, a_recv, g_send, g_recv, r_send, r_recv,
):
    tm, space = lax.axis_index("tm"), lax.axis_index("space")
    y, c = tm // 2, tm % 2
    z, x = space // 4, space % 4
    right = (tm, 4 * z + (x + 1) % 4)
    left = (tm, 4 * z + (x + 3) % 4)
    sibling = (2 * y + 1 - c, space)
    slot, core = z % 4, z // 4
    above, below = (space + 31) % 32, (space + 1) % 32
    later, earlier = (tm + 1) % 8, (tm + 7) % 8
    channels = feats_ref.shape[-1]

    def partner(i):
        return (2 * y + core, 4 * (4 * c + i) + x)

    def remote(i):
        return 4 * c + i != z

    weight_copies = [
        pltpu.make_async_copy(conv_hbm.at[lag], weight.at[lag], w_sem.at[lag]) for lag in range(3)]
    for copy in weight_copies:
        copy.start()

    barrier = pltpu.get_barrier_semaphore()
    for device in (
        left, right, sibling, (tm, above), (tm, below), (later, space), (earlier, space),
        (later, above), (later, below), (earlier, above), (earlier, below),
    ):
        pl.semaphore_signal(barrier, inc=1, device_id=device, device_id_type=MESH)
    for i in range(NB):
        @pl.when(remote(i))
        def _(i=i):
            pl.semaphore_signal(barrier, inc=1, device_id=partner(i), device_id_type=MESH)

    norm_gain = norm_gain_ref[...]
    for frame in range(NB):
        for row in range(2):
            unit = scaled(feats_ref[frame, row].astype(jnp.float32), norm_gain)
            active[frame + 2, row + 1] = (unit / (1.0 + jnp.exp(-unit))).astype(jnp.bfloat16)

    @pl.when(core == c)
    def _():
        pl.semaphore_wait(barrier, 14)

    @pl.when(core != c)
    def _():
        pl.semaphore_wait(barrier, 15)

    own, recent = pl.ds(2, NB), pl.ds(NB, 2)
    first = pl.ds(0, 2)
    has_above, has_below, has_earlier, has_later = space > 0, space < 31, tm > 0, tm < 7

    def rim(k, source, target, device):
        return pltpu.make_async_remote_copy(
            src_ref=active.at[source[0], source[1]], dst_ref=active.at[target[0], target[1]],
            send_sem=h_send.at[k], recv_sem=h_recv.at[k], device_id=device, device_id_type=MESH)

    top_row, low_row, both_rows = pl.ds(1, 1), pl.ds(2, 1), pl.ds(1, 2)
    before_row, after_row = pl.ds(0, 1), pl.ds(3, 1)
    rims = [
        (has_below, has_above, rim(0, (own, low_row), (own, before_row), (tm, below)), (own, before_row)),
        (has_above, has_below, rim(1, (own, top_row), (own, after_row), (tm, above)), (own, after_row)),
        (has_later, has_earlier, rim(2, (recent, both_rows), (first, both_rows), (later, space)), (first, both_rows)),
        (jnp.logical_and(has_later, has_below), jnp.logical_and(has_earlier, has_above),
         rim(3, (recent, low_row), (first, before_row), (later, below)), (first, before_row)),
        (jnp.logical_and(has_later, has_above), jnp.logical_and(has_earlier, has_below),
         rim(4, (recent, top_row), (first, after_row), (later, above)), (first, after_row)),
    ]
    for sends_it, gets_it, copy, place in rims:
        @pl.when(sends_it)
        def _(copy=copy):
            copy.start()

        @pl.when(jnp.logical_not(gets_it))
        def _(place=place):
            hole = active.at[place[0], place[1]]
            hole[...] = jnp.zeros_like(hole)

    column = lax.broadcasted_iota(jnp.int32, (COLS, channels), 0)

    def spread(frame, row):
        middle = active[frame, row]
        wide = middle.astype(jnp.float32)
        taps[frame, row, :, 0:channels] = jnp.where(
            column == 0, 0.0, pltpu.roll(wide, 1, 0)).astype(jnp.bfloat16)
        taps[frame, row, :, channels:2 * channels] = middle
        taps[frame, row, :, 2 * channels:3 * channels] = jnp.where(
            column == COLS - 1, 0.0, pltpu.roll(wide, COLS - 1, 0)).astype(jnp.bfloat16)

    def product(lag, offset, start, stop):
        window = taps[start + 2 - lag:stop + 2 - lag, offset:offset + 2]
        return jnp.dot(
            window.reshape((stop - start) * BLK, 3 * channels), weight[lag, offset],
            preferred_element_type=jnp.float32)

    lengths = [clip_ref[k] for k in range(3)]
    ends = [lengths[0], lengths[0] + lengths[1], lengths[0] + lengths[1] + lengths[2]]

    def live(frame, lag):
        at = tm * NB + frame
        start = jnp.int32(0)
        for length, end in zip(lengths, ends):
            start = start + jnp.where(end <= at, length, 0)
        return at - lag >= start

    def add(lag, value, start, stop):
        for frame in range(start, stop):
            part = value[(frame - start) * BLK:(frame - start + 1) * BLK]
            if lag:
                part = jnp.where(live(frame, lag), part, 0.0)
            conv[frame] += part

    for frame in range(2, NB + 2):
        for row in (1, 2):
            spread(frame, row)
    for frame in range(NB):
        conv[frame] = (
            feats_ref[frame].reshape(BLK, channels).astype(jnp.float32) + bias_ref[...])
    for lag in range(3):
        weight_copies[lag].wait()
        add(lag, product(lag, 1, lag, NB), lag, NB)

    def received(k):
        gets_it, copy = rims[k][1], rims[k][2]

        @pl.when(gets_it)
        def _():
            copy.wait_recv()

    received(0)
    received(1)
    for frame in range(2, NB + 2):
        for row in (0, 3):
            spread(frame, row)
    for lag in range(3):
        add(lag, product(lag, 0, lag, NB) + product(lag, 2, lag, NB), lag, NB)

    def exchange(i, source, target, send_sem, recv_sem):
        return pltpu.make_async_remote_copy(
            src_ref=source.at[i], dst_ref=target.at[slot], send_sem=send_sem.at[i],
            recv_sem=recv_sem.at[slot], device_id=partner(i), device_id_type=MESH)

    def arrival(b, target, send_sem, recv_sem):
        return pltpu.make_async_remote_copy(
            src_ref=target.at[b], dst_ref=target.at[b], send_sem=send_sem.at[b],
            recv_sem=recv_sem.at[b], device_id=partner(b), device_id_type=MESH)

    def hand_over(i):
        resid_ref[i] = conv[i].astype(jnp.bfloat16)

        @pl.when(remote(i))
        def _():
            exchange(i, resid_ref, rin, a_send, a_recv).start()

        @pl.when(jnp.logical_not(remote(i)))
        def _():
            rin[i] = resid_ref[i]

    hand_over(2)
    hand_over(3)
    for k in (2, 3, 4):
        received(k)
    for frame in range(2):
        for row in range(4):
            spread(frame, row)
    add(2, product(2, 0, 0, 2) + product(2, 1, 0, 2) + product(2, 2, 0, 2), 0, 2)
    add(1, product(1, 0, 0, 1) + product(1, 1, 0, 1) + product(1, 2, 0, 1), 0, 1)
    hand_over(0)
    hand_over(1)

    sends = []

    def push(source, dest, device):
        (sc, sp), (dc, dp) = source, dest
        copy = pltpu.make_async_remote_copy(
            src_ref=kv.at[sc, pl.ds(sp * BLK, BLK)], dst_ref=kv.at[dc, pl.ds(dp * BLK, BLK)],
            send_sem=g_send.at[len(sends)], recv_sem=g_recv.at[dc * NB + dp],
            device_id=device, device_id_type=MESH)
        copy.start()
        sends.append(copy)

    def landed(chunk, place):
        pltpu.make_async_remote_copy(
            src_ref=kv.at[chunk, pl.ds(place * BLK, BLK)], dst_ref=kv.at[chunk, pl.ds(place * BLK, BLK)],
            send_sem=g_send.at[0], recv_sem=g_recv.at[chunk * NB + place],
            device_id=sibling, device_id_type=MESH).wait_recv()

    for b in range(NB):
        @pl.when(remote(b))
        def _(b=b):
            arrival(b, rin, a_send, a_recv).wait_recv()

        kv[0, b * BLK:(b + 1) * BLK] = scaled(rin[b].astype(jnp.float32), gain_ref[...]).astype(jnp.bfloat16)
        push((0, b), (2 + b, 0), right)
        push((0, b), (2 + b, 1), left)
        push((0, b), (1, b), sibling)

    queries = jnp.dot(kv[0], wq_ref[...], preferred_element_type=jnp.float32).astype(jnp.bfloat16)
    folded = lax.dot_general(
        queries, wk_ref[...], (((1,), (1,)), ((), ())), preferred_element_type=jnp.float32)
    qs[...] = (folded * (math.log2(math.e) / math.sqrt(folded.shape[-1]))).astype(jnp.bfloat16)
    top[...] = jnp.full_like(top, -1e30)
    total[...] = jnp.zeros_like(total)
    acc[...] = jnp.zeros_like(acc)

    def attend(chunk, tile):
        at = pl.ds(pl.multiple_of(tile * TILE, TILE), TILE)
        keys = kv[chunk]
        scores = lax.dot_general(
            qs[at], keys, (((1,), (1,)), ((), ())), preferred_element_type=jnp.float32)
        old = top[at][:, :1]
        new = jnp.maximum(old, jnp.max(scores, axis=-1, keepdims=True))
        rescale = jnp.exp2(old - new)
        expanded = jnp.exp2(scores - new)
        parts = expanded[:, 0:128]
        for k in range(1, ROWS // 128):
            parts = parts + expanded[:, k * 128:(k + 1) * 128]
        total[at] = total[at] * rescale + parts
        acc[at] = acc[at] * rescale + jnp.dot(
            expanded.astype(jnp.bfloat16), keys, preferred_element_type=jnp.float32)
        top[at] = jnp.broadcast_to(new, (TILE, 128))

    def attend_all(chunk):
        def one(tile, carry):
            attend(chunk, tile)
            return carry
        lax.fori_loop(0, ROWS // TILE, one, 0)

    attend_all(0)
    for b in range(NB):
        landed(1, b)
    attend_all(1)
    for b in range(NB):
        landed(2 + b, 0)
        push((2 + b, 0), (2 + b, 2), sibling)
        if b < 2:
            push((2 + b, 0), (6, b), right)
        landed(2 + b, 1)
        push((2 + b, 1), (2 + b, 3), sibling)
        if b >= 2:
            push((2 + b, 1), (6, b), left)
        landed(2 + b, 2)
        landed(2 + b, 3)
        attend_all(2 + b)
    for b in range(NB):
        landed(6, b)
        push((6, b), (7, b), sibling)
    attend_all(6)
    for b in range(NB):
        landed(7, b)
    attend_all(7)

    for b in range(NB):
        rows = slice(b * BLK, (b + 1) * BLK)
        whole = jnp.sum(total[rows], axis=-1, keepdims=True)
        mixture = (acc[rows] / whole).astype(jnp.bfloat16)
        attended = jnp.dot(mixture, wv_ref[...], preferred_element_type=jnp.float32).astype(jnp.bfloat16)
        update = jnp.dot(attended, wo_ref[...], preferred_element_type=jnp.float32)
        stage[b] = (rin[b].astype(jnp.float32) + update).astype(jnp.bfloat16)

        @pl.when(remote(b))
        def _(b=b):
            exchange(b, stage, out_ref, r_send, r_recv).start()

        @pl.when(jnp.logical_not(remote(b)))
        def _(b=b):
            out_ref[b] = stage[b]

    for copy in sends:
        copy.wait_send()
    for sends_it, _, copy, _ in rims:
        @pl.when(sends_it)
        def _(copy=copy):
            copy.wait_send()
    for b in range(NB):
        @pl.when(remote(b))
        def _(b=b):
            exchange(b, resid_ref, rin, a_send, a_recv).wait_send()
            exchange(b, stage, out_ref, r_send, r_recv).wait_send()
            arrival(b, out_ref, r_send, r_recv).wait_recv()


def local(
    feats, clip_lengths, norm_gain, conv_weight, conv_bias, attn_gain,
    query_weight, key_weight, value_weight, output_weight,
):
    channels = feats.shape[-1]
    vmem = pl.BlockSpec(memory_space=pltpu.VMEM)
    smem = pl.BlockSpec(memory_space=pltpu.SMEM)
    hbm = pl.BlockSpec(memory_space=pl.ANY)
    dma = pltpu.SemaphoreType.DMA
    half = jax.ShapeDtypeStruct((NB, BLK, channels), jnp.bfloat16)
    resid, mixed = pl.pallas_call(
        block_kernel,
        out_shape=(half, half),
        in_specs=[vmem, smem, vmem, hbm] + [vmem] * 6,
        out_specs=(vmem, vmem),
        scratch_shapes=[
            pltpu.VMEM((3, 3, 3 * channels, channels), jnp.bfloat16),
            pltpu.VMEM((NB + 2, 4, COLS, channels), jnp.bfloat16),
            pltpu.VMEM((NB + 2, 4, COLS, 3 * channels), jnp.bfloat16),
            pltpu.VMEM((NB, BLK, channels), jnp.float32),
            pltpu.VMEM((NB, BLK, channels), jnp.bfloat16),
            pltpu.VMEM((8, ROWS, channels), jnp.bfloat16),
            pltpu.VMEM((ROWS, channels), jnp.bfloat16),
            pltpu.VMEM((ROWS, channels), jnp.float32),
            pltpu.VMEM((ROWS, 128), jnp.float32),
            pltpu.VMEM((ROWS, 128), jnp.float32),
            pltpu.VMEM((NB, BLK, channels), jnp.bfloat16),
            dma((3,)), dma((5,)), dma((5,)), dma((NB,)), dma((NB,)),
            dma((28,)), dma((32,)), dma((NB,)), dma((NB,)),
        ],
        compiler_params=pltpu.CompilerParams(
            collective_id=1, has_side_effects=True, vmem_limit_bytes=56 * 1024 * 1024),
        cost_estimate=pl.CostEstimate(
            flops=16_000_000_000, bytes_accessed=12_000_000, transcendentals=4_000_000),
    )(
        feats, clip_lengths, norm_gain.reshape(1, channels),
        conv_weight.reshape(3, 3, 3 * channels, channels), conv_bias.reshape(1, channels),
        attn_gain.reshape(1, channels), query_weight, key_weight, value_weight, output_weight,
    )
    return resid.reshape(feats.shape), mixed.reshape(feats.shape)


def solution(mesh):
    return jax.shard_map(
        local,
        mesh=mesh,
        in_specs=(P("tm", "space", None, None), P(), P(), P(), P(), P(), P(), P(), P(), P()),
        out_specs=(P("tm", "space", None, None), P("tm", "space", None, None)),
        check_vma=False,
    )
```

time: 351 us -> 82.9 us (0.24)
  the two profiles are of different devices: /device:TPU:41 before, /device:TPU:1 now
where the time goes in v1:
time: 82.9 us; the launch traced here: 82.7 us
  Pallas kernels  74.5 us (90%)
  local copies, waits for them, and re-layouts  7.47 us (9%)
    pallas_call x1, Pallas kernels, local(): pl.pallas_call(block_kernel, out_shape=(half, half), in_specs=[vmem, smem...  74.5 us
    unnamed x2, local copies, waits for them, and re-layouts  3.71 us

profile of v1, /device:TPU:1, one launch (start us, length us, event | category | flops | bytes accessed | tf_op | source)
XLA Modules:
  0.0 82.7 jit_solution(9871633873546056387)
XLA Ops:
  0.6 1.2 %reshape.22.norm_gain_ref = f32[1,384]{1,0:T(1,128)} reshape(f32[384]{0:T(512)} %param.12) | data formatting | bytes 3072 | tf_op jit(solution)/shard_map/reshape | solution.py:345
  1.9 1.2 %reshape.24.bias_ref = f32[1,384]{1,0:T(1,128)} reshape(f32[384]{0:T(512)} %param.14) | data formatting | bytes 3072 | tf_op jit(solution)/shard_map/reshape | solution.py:346
  3.1 1.3 %reshape.25.gain_ref = f32[1,384]{1,0:T(1,128)} reshape(f32[384]{0:T(512)} %param.15) | data formatting | bytes 3072 | tf_op jit(solution)/shard_map/reshape | solution.py:347
  4.4 74.5 %shard_map.113 = (bf16[4,160,384]{2,1,0:T(8,128)(2,1)}, bf16[4,160,384]{2,1,0:T(8,128)(2,1)}) custom-call(bf16[4,2,80,384]{3,2,1,0:T(8,128)(2,1)} %feats_ref.1, s32[3]{0:T(128)} %clip_ref.1, f32[1,384]{1,0:T(1,128)} %reshape.22.norm_gain_ref, bf16[3,3,1152,384]{3,2,1,0:T(8,128)(2,1)} %bitcast.5, f32[1,384]{1,0:T(1,128)} %reshape.24.bias_ref, ...), custom_call_target="tpu_custom_call" | custom-call | flops 16000000000 | bytes 12000000 | tf_op jit(solution)/shard_map/pallas_call | solution.py:320
  78.9 1.9 %copy.14 = bf16[4,2,80,384]{3,2,1,0:T(8,128)(2,1)} copy(bf16[4,2,80,384]{3,2,1,0:T(8,128)(2,1)} %bitcast.4) | data formatting | bytes 983040
  80.8 1.9 %copy.15 = bf16[4,2,80,384]{3,2,1,0:T(8,128)(2,1)} copy(bf16[4,2,80,384]{3,2,1,0:T(8,128)(2,1)} %bitcast.3) | data formatting | bytes 983040

commit v2 on v1

v2 whole, which is shorter than its diff:
```python
import math

import jax
import jax.numpy as jnp
from jax import lax
from jax.experimental import pallas as pl
from jax.experimental.pallas import tpu as pltpu
from jax.sharding import PartitionSpec as P

MESH = pl.DeviceIdType.MESH
COLS = 80
BLK = 2 * COLS
NB = 4
ROWS = NB * BLK
TILE = 320
PLACE = (1, 3, 0, 2)
FRAME = (2, 0, 3, 1)


def scaled(wide, gain):
    mean = jnp.mean(wide * wide, axis=-1, keepdims=True)
    return wide * lax.rsqrt(mean + 1e-06) * gain


def block_kernel(
    clip_ref, norm_gain_ref, bias_ref, gain_ref, feats_hbm, conv_hbm, wq_hbm, wk_hbm, wv_hbm, wo_hbm,
    resid_hbm, out_hbm,
    feats_ref, wq_ref, wk_ref, wv_ref, wo_ref,
    weight, active, taps, conv, resid_ref, rin, kv, qs, acc, top, total, stage,
    f_sem, p_sem, w_sem, o_sem, h_send, h_recv, a_send, a_recv, g_send, g_recv, r_send, r_recv,
):
    tm, space = lax.axis_index("tm"), lax.axis_index("space")
    y, c = tm // 2, tm % 2
    z, x = space // 4, space % 4
    right = (tm, 4 * z + (x + 1) % 4)
    left = (tm, 4 * z + (x + 3) % 4)
    sibling = (2 * y + 1 - c, space)
    slot, core = z % 4, z // 4
    above, below = (space + 31) % 32, (space + 1) % 32
    later, earlier = (tm + 1) % 8, (tm + 7) % 8
    channels = feats_ref.shape[-1]

    home_frame = slot // 2 + 2 * (1 - slot % 2)

    def partner(p):
        return (2 * y + core, 4 * (4 * c + p) + x)

    def remote(p):
        return 4 * c + p != z

    feats_copy = pltpu.make_async_copy(feats_hbm, feats_ref, f_sem)
    feats_copy.start()
    weight_copies = [
        pltpu.make_async_copy(conv_hbm.at[lag], weight.at[lag], w_sem.at[lag]) for lag in range(3)]
    small_copies = [
        pltpu.make_async_copy(source, target, p_sem.at[k])
        for k, (source, target) in enumerate(
            ((wq_hbm, wq_ref), (wk_hbm, wk_ref), (wv_hbm, wv_ref), (wo_hbm, wo_ref)))]
    for copy in weight_copies + small_copies:
        copy.start()

    barrier = pltpu.get_barrier_semaphore()
    for device in (
        left, right, sibling, (tm, above), (tm, below), (later, space), (earlier, space),
    ):
        pl.semaphore_signal(barrier, inc=1, device_id=device, device_id_type=MESH)
    for i in range(NB):
        @pl.when(remote(i))
        def _(i=i):
            pl.semaphore_signal(barrier, inc=1, device_id=partner(i), device_id_type=MESH)

    feats_copy.wait()
    norm_gain = norm_gain_ref[...].reshape(1, channels)
    attn_gain = gain_ref[...].reshape(1, channels)

    def activate(frame):
        for row in range(2):
            unit = scaled(feats_ref[frame, row].astype(jnp.float32), norm_gain)
            active[frame + 2, row + 1] = (unit / (1.0 + jnp.exp(-unit))).astype(jnp.bfloat16)

    for frame in (2, 3):
        activate(frame)

    @pl.when(core == c)
    def _():
        pl.semaphore_wait(barrier, 10)

    @pl.when(core != c)
    def _():
        pl.semaphore_wait(barrier, 11)

    older, recent = pl.ds(2, 2), pl.ds(4, 2)
    first = pl.ds(0, 2)
    has_above, has_below, has_earlier, has_later = space > 0, space < 31, tm > 0, tm < 7

    def rim(k, source, target, device):
        return pltpu.make_async_remote_copy(
            src_ref=active.at[source[0], source[1]], dst_ref=active.at[target[0], target[1]],
            send_sem=h_send.at[k], recv_sem=h_recv.at[k], device_id=device, device_id_type=MESH)

    top_row, low_row, both_rows = pl.ds(1, 1), pl.ds(2, 1), pl.ds(1, 2)
    before_row, after_row = pl.ds(0, 1), pl.ds(3, 1)
    rims = [
        (has_below, has_above, rim(0, (recent, low_row), (recent, before_row), (tm, below)), (recent, before_row)),
        (has_above, has_below, rim(1, (recent, top_row), (recent, after_row), (tm, above)), (recent, after_row)),
        (has_below, has_above, rim(2, (older, low_row), (older, before_row), (tm, below)), (older, before_row)),
        (has_above, has_below, rim(3, (older, top_row), (older, after_row), (tm, above)), (older, after_row)),
        (has_later, has_earlier, rim(4, (recent, both_rows), (first, both_rows), (later, space)), (first, both_rows)),
        (jnp.logical_and(has_later, has_above), jnp.logical_and(has_earlier, has_above),
         rim(5, (recent, before_row), (first, before_row), (later, space)), (first, before_row)),
        (jnp.logical_and(has_later, has_below), jnp.logical_and(has_earlier, has_below),
         rim(6, (recent, after_row), (first, after_row), (later, space)), (first, after_row)),
    ]

    def send_rim(k):
        @pl.when(rims[k][0])
        def _():
            rims[k][2].start()

    for k in (0, 1, 4):
        send_rim(k)
    for frame in (0, 1):
        activate(frame)
    for k in (2, 3):
        send_rim(k)
    for sends_it, gets_it, copy, place in rims:
        @pl.when(jnp.logical_not(gets_it))
        def _(place=place):
            hole = active.at[place[0], place[1]]
            hole[...] = jnp.zeros_like(hole)

    column = lax.broadcasted_iota(jnp.int32, (COLS, channels), 0)

    def spread(frame, row):
        middle = active[frame, row]
        wide = middle.astype(jnp.float32)
        taps[frame, row, :, 0:channels] = jnp.where(
            column == 0, 0.0, pltpu.roll(wide, 1, 0)).astype(jnp.bfloat16)
        taps[frame, row, :, channels:2 * channels] = middle
        taps[frame, row, :, 2 * channels:3 * channels] = jnp.where(
            column == COLS - 1, 0.0, pltpu.roll(wide, COLS - 1, 0)).astype(jnp.bfloat16)

    def product(lag, offset, start, stop):
        window = taps[start + 2 - lag:stop + 2 - lag, offset:offset + 2]
        return jnp.dot(
            window.reshape((stop - start) * BLK, 3 * channels), weight[lag, offset],
            preferred_element_type=jnp.float32)

    lengths = [clip_ref[k] for k in range(3)]
    ends = [lengths[0], lengths[0] + lengths[1], lengths[0] + lengths[1] + lengths[2]]

    def live(frame, lag):
        at = tm * NB + frame
        start = jnp.int32(0)
        for length, end in zip(lengths, ends):
            start = start + jnp.where(end <= at, length, 0)
        return at - lag >= start

    def add(lag, value, start, stop):
        for frame in range(start, stop):
            part = value[(frame - start) * BLK:(frame - start + 1) * BLK]
            if lag:
                part = jnp.where(live(frame, lag), part, 0.0)
            conv[frame] += part

    for frame in (4, 5, 3, 2):
        for row in (1, 2):
            spread(frame, row)
    for frame in range(NB):
        conv[frame] = (
            feats_ref[frame].reshape(BLK, channels).astype(jnp.float32) + bias_ref[...].reshape(1, channels))
    weight_copies[0].wait()
    add(0, product(0, 1, 0, NB), 0, NB)
    for lag in (1, 2):
        weight_copies[lag].wait()
        add(lag, product(lag, 1, 2, NB), 2, NB)

    def received(k):
        gets_it, copy = rims[k][1], rims[k][2]

        @pl.when(gets_it)
        def _():
            copy.wait_recv()

    for k in (0, 1):
        received(k)
        send_rim(k + 5)
    for frame in (4, 5):
        for row in (0, 3):
            spread(frame, row)
    add(0, product(0, 0, 2, NB) + product(0, 2, 2, NB), 2, NB)
    for k in (2, 3):
        received(k)
    for frame in (2, 3):
        for row in (0, 3):
            spread(frame, row)
    for lag in (1, 2):
        add(lag, product(lag, 0, 2, NB) + product(lag, 2, 2, NB), 2, NB)

    def dispatch(i):
        return pltpu.make_async_remote_copy(
            src_ref=resid_ref.at[i], dst_ref=rin.at[slot], send_sem=a_send.at[i],
            recv_sem=a_recv.at[slot], device_id=partner(PLACE[i]), device_id_type=MESH)

    def bring_back(b):
        return pltpu.make_async_remote_copy(
            src_ref=stage.at[b], dst_ref=out_hbm.at[home_frame], send_sem=r_send.at[b],
            recv_sem=r_recv.at[home_frame], device_id=partner(b), device_id_type=MESH)

    def arrival(k, target, recv_sem):
        return pltpu.make_async_remote_copy(
            src_ref=target.at[k], dst_ref=target.at[k], send_sem=a_send.at[k],
            recv_sem=recv_sem.at[k], device_id=sibling, device_id_type=MESH)

    resid_copies = [
        pltpu.make_async_copy(resid_ref.at[i], resid_hbm.at[i], o_sem.at[i]) for i in range(NB)]

    def hand_over(i):
        resid_ref[i] = conv[i].astype(jnp.bfloat16)
        resid_copies[i].start()

        @pl.when(remote(PLACE[i]))
        def _():
            dispatch(i).start()

        @pl.when(jnp.logical_not(remote(PLACE[i])))
        def _():
            rin[PLACE[i]] = resid_ref[i]

    hand_over(2)
    hand_over(3)
    add(0, product(0, 0, 0, 2) + product(0, 2, 0, 2), 0, 2)
    for k in (4, 5, 6):
        received(k)
    for frame in range(2):
        for row in range(4):
            spread(frame, row)
    for lag in (1, 2):
        add(lag, product(lag, 0, 0, 2) + product(lag, 1, 0, 2) + product(lag, 2, 0, 2), 0, 2)
    hand_over(0)
    hand_over(1)

    sends = []

    def block(group, place):
        return kv.at[group, pl.ds(place * BLK, BLK)]

    def push(source, dest, device):
        copy = pltpu.make_async_remote_copy(
            src_ref=block(*source), dst_ref=block(*dest),
            send_sem=g_send.at[len(sends)], recv_sem=g_recv.at[dest[0] * 8 + dest[1]],
            device_id=device, device_id_type=MESH)
        copy.start()
        sends.append(copy)

    def landed(group, place):
        pltpu.make_async_remote_copy(
            src_ref=block(group, place), dst_ref=block(group, place),
            send_sem=g_send.at[0], recv_sem=g_recv.at[group * 8 + place],
            device_id=sibling, device_id_type=MESH).wait_recv()

    home = {0: (1, 0), 2: (1, 1), 1: (2, 0), 3: (2, 1)}

    def normalise(b):
        @pl.when(remote(b))
        def _():
            arrival(b, rin, a_recv).wait_recv()

        kv[0, b * BLK:(b + 1) * BLK] = scaled(rin[b].astype(jnp.float32), attn_gain).astype(jnp.bfloat16)

    for b, other in ((0, 2), (1, 3)):
        normalise(b)
        normalise(other)
        for to_right, to_left in ((b, other), (other, b)):
            group, place = home[to_right]
            push((0, to_right), (group, place), right)
            group, place = home[to_left]
            push((0, to_left), (group, 2 + place), left)
        for own_block in (b, other):
            push((0, own_block), (0, 4 + own_block), sibling)

    for copy in small_copies:
        copy.wait()
    queries = jnp.dot(kv[0, 0:ROWS], wq_ref[...], preferred_element_type=jnp.float32).astype(jnp.bfloat16)
    folded = lax.dot_general(
        queries, wk_ref[...], (((1,), (1,)), ((), ())), preferred_element_type=jnp.float32)
    qs[...] = (folded * (math.log2(math.e) / math.sqrt(folded.shape[-1]))).astype(jnp.bfloat16)
    top[...] = jnp.full_like(top, -1e30)
    total[...] = jnp.zeros_like(total)
    acc[...] = jnp.zeros_like(acc)

    def attend(group, tile, begin=0, end=2 * ROWS):
        at = slice(tile * TILE, (tile + 1) * TILE)
        keys = kv[group, begin:end]
        scores = lax.dot_general(
            qs[at], keys, (((1,), (1,)), ((), ())), preferred_element_type=jnp.float32)
        pieces = [scores[:, k:k + 128] for k in range(0, end - begin, 128)]
        lanes = pieces[0]
        for piece in pieces[1:]:
            lanes = jnp.maximum(lanes, piece)
        old = top[at]
        new = jnp.maximum(old, jnp.broadcast_to(jnp.max(lanes, axis=-1, keepdims=True), old.shape))
        rescale = jnp.exp2(old - new)
        expanded = [jnp.exp2(piece - new) for piece in pieces]
        parts = expanded[0]
        for piece in expanded[1:]:
            parts = parts + piece
        total[at] = total[at] * rescale + parts
        top[at] = new
        weights = jnp.concatenate([piece.astype(jnp.bfloat16) for piece in expanded], axis=1)
        summed = jnp.dot(weights, keys, preferred_element_type=jnp.float32)
        for k in range(0, channels, 128):
            acc[at, k:k + 128] = acc[at, k:k + 128] * rescale + summed[:, k:k + 128]

    tiles = range(ROWS // TILE)
    for b in range(NB):
        landed(0, 4 + b)
    for tile in tiles:
        attend(0, tile)
    for group, from_left, from_right in ((1, 0, 2), (2, 1, 3)):
        for place, forward, device in ((0, from_left, right), (3, from_right, left), (1, None, None), (2, None, None)):
            landed(group, place)
            if forward is not None:
                push((group, place), (3, forward), device)
            push((group, place), (group, 4 + place), sibling)
        for place in range(4):
            landed(group, 4 + place)
        for tile in tiles:
            attend(group, tile)
    for b in (0, 2, 1, 3):
        landed(3, b)
        push((3, b), (3, 4 + b), sibling)
    for tile in tiles:
        attend(3, tile, 0, ROWS)
    for b in range(NB):
        landed(3, 4 + b)

    for tile in tiles:
        attend(3, tile, ROWS, 2 * ROWS)
        at = slice(tile * TILE, (tile + 1) * TILE)
        whole = jnp.sum(total[at], axis=-1, keepdims=True)
        mixture = (acc[at] / whole).astype(jnp.bfloat16)
        attended = jnp.dot(mixture, wv_ref[...], preferred_element_type=jnp.float32).astype(jnp.bfloat16)
        update = jnp.dot(attended, wo_ref[...], preferred_element_type=jnp.float32)
        for half in range(TILE // BLK):
            b = tile * (TILE // BLK) + half
            stage[b] = (
                rin[b].astype(jnp.float32) + update[half * BLK:(half + 1) * BLK]).astype(jnp.bfloat16)

            @pl.when(remote(b))
            def _(b=b):
                bring_back(b).start()

            @pl.when(jnp.logical_not(remote(b)))
            def _(b=b):
                pltpu.make_async_copy(stage.at[b], out_hbm.at[FRAME[b]], o_sem.at[NB]).start()

    for copy in sends:
        copy.wait_send()
    for sends_it, _, copy, _ in rims:
        @pl.when(sends_it)
        def _(copy=copy):
            copy.wait_send()
    for b in range(NB):
        @pl.when(remote(b))
        def _(b=b):
            dispatch(FRAME[b]).wait_send()
            bring_back(b).wait_send()
            arrival(FRAME[b], out_hbm, r_recv).wait_recv()

        @pl.when(jnp.logical_not(remote(b)))
        def _(b=b):
            pltpu.make_async_copy(stage.at[b], out_hbm.at[FRAME[b]], o_sem.at[NB]).wait()
        resid_copies[b].wait()


def finish_kernel(resid_ref, mixed_ref, resid_out, mixed_out, held, in_sems, out_sems):
    pairs = [(resid_ref, resid_out), (mixed_ref, mixed_out)]
    fetched = [pltpu.make_async_copy(pairs[k][0], held.at[k], in_sems.at[k]) for k in range(2)]
    stored = [pltpu.make_async_copy(held.at[k], pairs[k][1], out_sems.at[k]) for k in range(2)]
    for copy in fetched:
        copy.start()
    for first, second in zip(fetched, stored):
        first.wait()
        second.start()
    for copy in stored:
        copy.wait()


def local(
    feats, clip_lengths, norm_gain, conv_weight, conv_bias, attn_gain,
    query_weight, key_weight, value_weight, output_weight,
):
    channels = feats.shape[-1]
    vmem = pl.BlockSpec(memory_space=pltpu.VMEM)
    smem = pl.BlockSpec(memory_space=pltpu.SMEM)
    hbm = pl.BlockSpec(memory_space=pl.ANY)
    dma = pltpu.SemaphoreType.DMA
    half = jax.ShapeDtypeStruct((NB, BLK, channels), jnp.bfloat16)
    resid, mixed = pl.pallas_call(
        block_kernel,
        out_shape=(half, half),
        in_specs=[smem] + [vmem] * 3 + [hbm] * 6,
        out_specs=(hbm, hbm),
        scratch_shapes=[
            pltpu.VMEM(feats.shape, jnp.bfloat16),
        ] + [pltpu.VMEM((channels, channels), jnp.bfloat16)] * 4 + [
            pltpu.VMEM((3, 3, 3 * channels, channels), jnp.bfloat16),
            pltpu.VMEM((NB + 2, 4, COLS, channels), jnp.bfloat16),
            pltpu.VMEM((NB + 2, 4, COLS, 3 * channels), jnp.bfloat16),
            pltpu.VMEM((NB, BLK, channels), jnp.float32),
            pltpu.VMEM((NB, BLK, channels), jnp.bfloat16),
            pltpu.VMEM((NB, BLK, channels), jnp.bfloat16),
            pltpu.VMEM((4, 2 * ROWS, channels), jnp.bfloat16),
            pltpu.VMEM((ROWS, channels), jnp.bfloat16),
            pltpu.VMEM((ROWS, channels), jnp.float32),
            pltpu.VMEM((ROWS, 128), jnp.float32),
            pltpu.VMEM((ROWS, 128), jnp.float32),
            pltpu.VMEM((NB, BLK, channels), jnp.bfloat16),
            dma, dma((4,)), dma((3,)), dma((NB + 1,)), dma((7,)), dma((7,)), dma((NB,)), dma((NB,)),
            dma((28,)), dma((32,)), dma((NB,)), dma((NB,)),
        ],
        compiler_params=pltpu.CompilerParams(
            collective_id=1, has_side_effects=True, vmem_limit_bytes=56 * 1024 * 1024),
        cost_estimate=pl.CostEstimate(
            flops=16_000_000_000, bytes_accessed=12_000_000, transcendentals=4_000_000),
    )(
        clip_lengths, norm_gain, conv_bias, attn_gain, feats,
        conv_weight.reshape(3, 3, 3 * channels, channels),
        query_weight, key_weight, value_weight, output_weight,
    )
    resid, mixed = pl.pallas_call(
        finish_kernel,
        out_shape=(half, half),
        in_specs=[hbm, hbm],
        out_specs=(hbm, hbm),
        scratch_shapes=[pltpu.VMEM((2, NB, BLK, channels), jnp.bfloat16), dma((2,)), dma((2,))],
        compiler_params=pltpu.CompilerParams(vmem_limit_bytes=60 * 1024 * 1024),
    )(resid, mixed)
    return resid.reshape(feats.shape), mixed.reshape(feats.shape)


def solution(mesh):
    return jax.shard_map(
        local,
        mesh=mesh,
        in_specs=(P("tm", "space", None, None), P(), P(), P(), P(), P(), P(), P(), P(), P()),
        out_specs=(P("tm", "space", None, None), P("tm", "space", None, None)),
        check_vma=False,
    )
```

time: 82.9 us -> 65.9 us (0.79)
  the two profiles are of different devices: /device:TPU:1 before, /device:TPU:41 now
where the time goes in v2:
time: 65.9 us; the launch traced here: 64.9 us
  Pallas kernels  64.1 us (97%)
  between operations  0.8 us (1%)
    pallas_call x1, Pallas kernels, local(): pl.pallas_call(block_kernel, out_shape=(half, half), in_specs=[smem] + [v...  62.1 us
    pallas_call x1, Pallas kernels, local(): pl.pallas_call(finish_kernel, out_shape=(half, half), in_specs=[hbm, hbm]...  2 us

profile of v2, /device:TPU:41, one launch (start us, length us, event | category | flops | bytes accessed | tf_op | source)
XLA Modules:
  0.0 64.9 jit_solution(13517685572361610349)
XLA Ops:
  0.6 62.1 %shard_map.113 = (bf16[4,160,384]{2,1,0:T(8,128)(2,1)}, bf16[4,160,384]{2,1,0:T(8,128)(2,1)}) custom-call(s32[3]{0:T(128)} %clip_ref.1, f32[384]{0:T(512)} %norm_gain_ref.1, f32[384]{0:T(512)} %bias_ref.1, f32[384]{0:T(512)} %gain_ref.1, bf16[4,2,80,384]{3,2,1,0:T(8,128)(2,1)} %feats_hbm.1, bf16[3,3,1152,384]{3,2,1,0:T(8,128)(2,1)} %bitcast.3, ...), custom_call_target="tpu_custom_call" | custom-call | flops 16000000000 | bytes 12000000 | tf_op jit(solution)/shard_map/pallas_call | solution.py:400
  62.8 2.0 %shard_map.114 = (bf16[4,160,384]{2,1,0:T(8,128)(2,1)}, bf16[4,160,384]{2,1,0:T(8,128)(2,1)}) custom-call(bf16[4,160,384]{2,1,0:T(8,128)(2,1)} %get-tuple-element.6.resid_ref, bf16[4,160,384]{2,1,0:T(8,128)(2,1)} %get-tuple-element.7.mixed_ref), custom_call_target="tpu_custom_call" | custom-call | tf_op jit(solution)/shard_map/pallas_call | solution.py:432

commit v3 on v2

--- a/solution.py
+++ b/solution.py
@@ -15,6 +15,7 @@
 TILE = 320
 PLACE = (1, 3, 0, 2)
 FRAME = (2, 0, 3, 1)
+TURN = (0, 2, 1, 3)
 
 
 def scaled(wide, gain):
@@ -48,6 +49,12 @@
     def remote(p):
         return 4 * c + p != z
 
+    away, step = (core + c) % 2, 1 - 2 * (slot // 2)
+
+    def origin(l):
+        turn = TURN[l] + away * (3 - 2 * TURN[l])
+        return (slot + step * turn + 8) % 4
+
     feats_copy = pltpu.make_async_copy(feats_hbm, feats_ref, f_sem)
     feats_copy.start()
     weight_copies = [
@@ -202,10 +209,13 @@
             src_ref=resid_ref.at[i], dst_ref=rin.at[slot], send_sem=a_send.at[i],
             recv_sem=a_recv.at[slot], device_id=partner(PLACE[i]), device_id_type=MESH)
 
-    def bring_back(b):
+    def bring_back(l):
         return pltpu.make_async_remote_copy(
-            src_ref=stage.at[b], dst_ref=out_hbm.at[home_frame], send_sem=r_send.at[b],
-            recv_sem=r_recv.at[home_frame], device_id=partner(b), device_id_type=MESH)
+            src_ref=stage.at[l], dst_ref=out_hbm.at[home_frame], send_sem=r_send.at[l],
+            recv_sem=r_recv.at[home_frame], device_id=partner(origin(l)), device_id_type=MESH)
+
+    def put_back(l):
+        return pltpu.make_async_copy(stage.at[l], out_hbm.at[home_frame], o_sem.at[NB])
 
     def arrival(k, target, recv_sem):
         return pltpu.make_async_remote_copy(
@@ -261,23 +271,21 @@
 
     home = {0: (1, 0), 2: (1, 1), 1: (2, 0), 3: (2, 1)}
 
-    def normalise(b):
+    def normalise(l):
+        b = origin(l)
+
         @pl.when(remote(b))
         def _():
             arrival(b, rin, a_recv).wait_recv()
 
-        kv[0, b * BLK:(b + 1) * BLK] = scaled(rin[b].astype(jnp.float32), attn_gain).astype(jnp.bfloat16)
-
-    for b, other in ((0, 2), (1, 3)):
-        normalise(b)
-        normalise(other)
-        for to_right, to_left in ((b, other), (other, b)):
-            group, place = home[to_right]
-            push((0, to_right), (group, place), right)
-            group, place = home[to_left]
-            push((0, to_left), (group, 2 + place), left)
-        for own_block in (b, other):
-            push((0, own_block), (0, 4 + own_block), sibling)
+        kv[0, l * BLK:(l + 1) * BLK] = scaled(rin[b].astype(jnp.float32), attn_gain).astype(jnp.bfloat16)
+        group, place = home[l]
+        push((0, l), (group, place), right)
+        push((0, l), (group, 2 + place), left)
+        push((0, l), (0, 4 + l), sibling)
+
+    for l in TURN:
+        normalise(l)
 
     for copy in small_copies:
         copy.wait()
@@ -343,17 +351,17 @@
         attended = jnp.dot(mixture, wv_ref[...], preferred_element_type=jnp.float32).astype(jnp.bfloat16)
         update = jnp.dot(attended, wo_ref[...], preferred_element_type=jnp.float32)
         for half in range(TILE // BLK):
-            b = tile * (TILE // BLK) + half
-            stage[b] = (
-                rin[b].astype(jnp.float32) + update[half * BLK:(half + 1) * BLK]).astype(jnp.bfloat16)
-
-            @pl.when(remote(b))
-            def _(b=b):
-                bring_back(b).start()
-
-            @pl.when(jnp.logical_not(remote(b)))
-            def _(b=b):
-                pltpu.make_async_copy(stage.at[b], out_hbm.at[FRAME[b]], o_sem.at[NB]).start()
+            l = tile * (TILE // BLK) + half
+            stage[l] = (
+                rin[origin(l)].astype(jnp.float32) + update[half * BLK:(half + 1) * BLK]).astype(jnp.bfloat16)
+
+            @pl.when(remote(origin(l)))
+            def _(l=l):
+                bring_back(l).start()
+
+            @pl.when(jnp.logical_not(remote(origin(l))))
+            def _(l=l):
+                put_back(l).start()
 
     for copy in sends:
         copy.wait_send()
@@ -365,12 +373,15 @@
         @pl.when(remote(b))
         def _(b=b):
             dispatch(FRAME[b]).wait_send()
+            arrival(FRAME[b], out_hbm, r_recv).wait_recv()
+
+        @pl.when(remote(origin(b)))
+        def _(b=b):
             bring_back(b).wait_send()
-            arrival(FRAME[b], out_hbm, r_recv).wait_recv()
-
-        @pl.when(jnp.logical_not(remote(b)))
+
+        @pl.when(jnp.logical_not(remote(origin(b))))
         def _(b=b):
-            pltpu.make_async_copy(stage.at[b], out_hbm.at[FRAME[b]], o_sem.at[NB]).wait()
+            put_back(b).wait()
         resid_copies[b].wait()
 
 

time: 65.9 us -> 66 us (level); the launches traced: 64.9 us -> 65.9 us
  Pallas kernels: 64.1 us -> 65.1 us
    pallas_call x1, Pallas kernels: 62.1 us -> 63 us  [local(): pl.pallas_call(block_kernel, out_shape=(half, half), in_specs=[smem] + [v...]
where the time goes in v3:
time: 66 us; the launch traced here: 65.9 us
  Pallas kernels  65.1 us (99%)
  between operations  0.8 us (1%)
    pallas_call x1, Pallas kernels, local(): pl.pallas_call(block_kernel, out_shape=(half, half), in_specs=[smem] + [v...  63 us
    pallas_call x1, Pallas kernels, local(): pl.pallas_call(finish_kernel, out_shape=(half, half), in_specs=[hbm, hbm]...  2 us

profile of v3, /device:TPU:41, one launch (start us, length us, event | category | flops | bytes accessed | tf_op | source)
XLA Modules:
  0.0 65.9 jit_solution(12665061396656712240)
XLA Ops:
  0.6 63.0 %shard_map.113 = (bf16[4,160,384]{2,1,0:T(8,128)(2,1)}, bf16[4,160,384]{2,1,0:T(8,128)(2,1)}) custom-call(s32[3]{0:T(128)} %clip_ref.1, f32[384]{0:T(512)} %norm_gain_ref.1, f32[384]{0:T(512)} %bias_ref.1, f32[384]{0:T(512)} %gain_ref.1, bf16[4,2,80,384]{3,2,1,0:T(8,128)(2,1)} %feats_hbm.1, bf16[3,3,1152,384]{3,2,1,0:T(8,128)(2,1)} %bitcast.3, ...), custom_call_target="tpu_custom_call" | custom-call | flops 16000000000 | bytes 12000000 | tf_op jit(solution)/shard_map/pallas_call | solution.py:411
  63.7 2.0 %shard_map.114 = (bf16[4,160,384]{2,1,0:T(8,128)(2,1)}, bf16[4,160,384]{2,1,0:T(8,128)(2,1)}) custom-call(bf16[4,160,384]{2,1,0:T(8,128)(2,1)} %get-tuple-element.6.resid_ref, bf16[4,160,384]{2,1,0:T(8,128)(2,1)} %get-tuple-element.7.mixed_ref), custom_call_target="tpu_custom_call" | custom-call | tf_op jit(solution)/shard_map/pallas_call | solution.py:443

commit v4 on v3

--- a/solution.py
+++ b/solution.py
@@ -13,7 +13,6 @@
 NB = 4
 ROWS = NB * BLK
 TILE = 320
-PLACE = (1, 3, 0, 2)
 FRAME = (2, 0, 3, 1)
 TURN = (0, 2, 1, 3)
 
@@ -49,11 +48,16 @@
     def remote(p):
         return 4 * c + p != z
 
-    away, step = (core + c) % 2, 1 - 2 * (slot // 2)
+    away, odd, high = (core + c) % 2, slot % 2, slot // 2
+    near = (high + away) % 2
+    first_near = (1 - away) * odd + away * (1 - high)
+    first_far = (1 - away) * high + away * (1 - odd)
+    order = (
+        2 * near + first_near, 2 * near + 1 - first_near,
+        2 * (1 - near) + first_far, 2 * (1 - near) + 1 - first_far)
 
     def origin(l):
-        turn = TURN[l] + away * (3 - 2 * TURN[l])
-        return (slot + step * turn + 8) % 4
+        return order[TURN[l]]
 
     feats_copy = pltpu.make_async_copy(feats_hbm, feats_ref, f_sem)
     feats_copy.start()
@@ -204,10 +208,10 @@
     for lag in (1, 2):
         add(lag, product(lag, 0, 2, NB) + product(lag, 2, 2, NB), 2, NB)
 
-    def dispatch(i):
+    def dispatch(i, p):
         return pltpu.make_async_remote_copy(
             src_ref=resid_ref.at[i], dst_ref=rin.at[slot], send_sem=a_send.at[i],
-            recv_sem=a_recv.at[slot], device_id=partner(PLACE[i]), device_id_type=MESH)
+            recv_sem=a_recv.at[slot], device_id=partner(p), device_id_type=MESH)
 
     def bring_back(l):
         return pltpu.make_async_remote_copy(
@@ -225,21 +229,24 @@
     resid_copies = [
         pltpu.make_async_copy(resid_ref.at[i], resid_hbm.at[i], o_sem.at[i]) for i in range(NB)]
 
-    def hand_over(i):
+    def settle(i):
         resid_ref[i] = conv[i].astype(jnp.bfloat16)
         resid_copies[i].start()
 
-        @pl.when(remote(PLACE[i]))
+    def hand_over(i, p):
+        @pl.when(remote(p))
         def _():
-            dispatch(i).start()
-
-        @pl.when(jnp.logical_not(remote(PLACE[i])))
+            dispatch(i, p).start()
+
+        @pl.when(jnp.logical_not(remote(p)))
         def _():
-            rin[PLACE[i]] = resid_ref[i]
-
-    hand_over(2)
-    hand_over(3)
+            rin[slot] = resid_ref[i]
+
+    for i in (2, 3):
+        settle(i)
+    hand_over(2 + near, 2 * near)
     add(0, product(0, 0, 0, 2) + product(0, 2, 0, 2), 0, 2)
+    hand_over(3 - near, 2 - 2 * near)
     for k in (4, 5, 6):
         received(k)
     for frame in range(2):
@@ -247,8 +254,9 @@
             spread(frame, row)
     for lag in (1, 2):
         add(lag, product(lag, 0, 0, 2) + product(lag, 1, 0, 2) + product(lag, 2, 0, 2), 0, 2)
-    hand_over(0)
-    hand_over(1)
+    for i in (0, 1):
+        settle(i)
+    hand_over(near, 1 + 2 * near)
 
     sends = []
 
@@ -284,7 +292,15 @@
         push((0, l), (group, 2 + place), left)
         push((0, l), (0, 4 + l), sibling)
 
-    for l in TURN:
+    for l in (0, 2):
+        normalise(l)
+
+    @pl.when(remote(1 + 2 * near))
+    def _():
+        dispatch(near, 1 + 2 * near).wait_send()
+
+    hand_over(1 - near, 3 - 2 * near)
+    for l in (1, 3):
         normalise(l)
 
     for copy in small_copies:
@@ -321,20 +337,28 @@
             acc[at, k:k + 128] = acc[at, k:k + 128] * rescale + summed[:, k:k + 128]
 
     tiles = range(ROWS // TILE)
-    for b in range(NB):
-        landed(0, 4 + b)
-    for tile in tiles:
-        attend(0, tile)
-    for group, from_left, from_right in ((1, 0, 2), (2, 1, 3)):
+
+    def relay(group, from_left, from_right):
         for place, forward, device in ((0, from_left, right), (3, from_right, left), (1, None, None), (2, None, None)):
             landed(group, place)
             if forward is not None:
                 push((group, place), (3, forward), device)
             push((group, place), (group, 4 + place), sibling)
-        for place in range(4):
-            landed(group, 4 + place)
-        for tile in tiles:
-            attend(group, tile)
+
+    relay(1, 0, 2)
+    for b in range(NB):
+        landed(0, 4 + b)
+    for tile in tiles:
+        attend(0, tile)
+    for place in range(4):
+        landed(1, 4 + place)
+    for tile in tiles:
+        attend(1, tile)
+    relay(2, 1, 3)
+    for place in range(4):
+        landed(2, 4 + place)
+    for tile in tiles:
+        attend(2, tile)
     for b in (0, 2, 1, 3):
         landed(3, b)
         push((3, b), (3, 4 + b), sibling)
@@ -369,10 +393,13 @@
         @pl.when(sends_it)
         def _(copy=copy):
             copy.wait_send()
+    for i, p in ((2 + near, 2 * near), (3 - near, 2 - 2 * near), (1 - near, 3 - 2 * near)):
+        @pl.when(remote(p))
+        def _(i=i, p=p):
+            dispatch(i, p).wait_send()
     for b in range(NB):
         @pl.when(remote(b))
         def _(b=b):
-            dispatch(FRAME[b]).wait_send()
             arrival(FRAME[b], out_hbm, r_recv).wait_recv()
 
         @pl.when(remote(origin(b)))

time: 66 us -> 68.6 us (1.039)
  Pallas kernels: 65.1 us -> 67.4 us
    pallas_call x1, Pallas kernels: 63 us -> 65.4 us  [local(): pl.pallas_call(block_kernel, out_shape=(half, half), in_specs=[smem] + [v...]
where the time goes in v4:
time: 68.6 us; the launch traced here: 68.2 us
  Pallas kernels  67.4 us (98%)
  between operations  0.8 us (1%)
    pallas_call x1, Pallas kernels, local(): pl.pallas_call(block_kernel, out_shape=(half, half), in_specs=[smem] + [v...  65.4 us
    pallas_call x1, Pallas kernels, local(): pl.pallas_call(finish_kernel, out_shape=(half, half), in_specs=[hbm, hbm]...  2 us

profile of v4, /device:TPU:41, one launch (start us, length us, event | category | flops | bytes accessed | tf_op | source)
XLA Modules:
  0.0 68.2 jit_solution(11570330253960727446)
XLA Ops:
  0.6 65.4 %shard_map.113 = (bf16[4,160,384]{2,1,0:T(8,128)(2,1)}, bf16[4,160,384]{2,1,0:T(8,128)(2,1)}) custom-call(s32[3]{0:T(128)} %clip_ref.1, f32[384]{0:T(512)} %norm_gain_ref.1, f32[384]{0:T(512)} %bias_ref.1, f32[384]{0:T(512)} %gain_ref.1, bf16[4,2,80,384]{3,2,1,0:T(8,128)(2,1)} %feats_hbm.1, bf16[3,3,1152,384]{3,2,1,0:T(8,128)(2,1)} %bitcast.3, ...), custom_call_target="tpu_custom_call" | custom-call | flops 16000000000 | bytes 12000000 | tf_op jit(solution)/shard_map/pallas_call | solution.py:438
  66.1 2.0 %shard_map.114 = (bf16[4,160,384]{2,1,0:T(8,128)(2,1)}, bf16[4,160,384]{2,1,0:T(8,128)(2,1)}) custom-call(bf16[4,160,384]{2,1,0:T(8,128)(2,1)} %get-tuple-element.6.resid_ref, bf16[4,160,384]{2,1,0:T(8,128)(2,1)} %get-tuple-element.7.mixed_ref), custom_call_target="tpu_custom_call" | custom-call | tf_op jit(solution)/shard_map/pallas_call | solution.py:470

commit v5 on v3

--- a/solution.py
+++ b/solution.py
@@ -338,12 +338,13 @@
     for b in (0, 2, 1, 3):
         landed(3, b)
         push((3, b), (3, 4 + b), sibling)
-    for tile in tiles:
-        attend(3, tile, 0, ROWS)
+    attend(3, 0, 0, ROWS)
     for b in range(NB):
         landed(3, 4 + b)
 
     for tile in tiles:
+        if tile:
+            attend(3, tile, 0, ROWS)
         attend(3, tile, ROWS, 2 * ROWS)
         at = slice(tile * TILE, (tile + 1) * TILE)
         whole = jnp.sum(total[at], axis=-1, keepdims=True)

time: 66 us -> 65.8 us (level)
  no operation moved by 1% of the time
where the time goes in v5:
time: 65.8 us; the launch traced here: 65.7 us
  Pallas kernels  64.9 us (99%)
  between operations  0.8 us (1%)
    pallas_call x1, Pallas kernels, local(): pl.pallas_call(block_kernel, out_shape=(half, half), in_specs=[smem] + [v...  62.9 us
    pallas_call x1, Pallas kernels, local(): pl.pallas_call(finish_kernel, out_shape=(half, half), in_specs=[hbm, hbm]...  2 us

profile of v5, /device:TPU:41, one launch (start us, length us, event | category | flops | bytes accessed | tf_op | source)
XLA Modules:
  0.0 65.7 jit_solution(16056607394355012912)
XLA Ops:
  0.6 62.9 %shard_map.113 = (bf16[4,160,384]{2,1,0:T(8,128)(2,1)}, bf16[4,160,384]{2,1,0:T(8,128)(2,1)}) custom-call(s32[3]{0:T(128)} %clip_ref.1, f32[384]{0:T(512)} %norm_gain_ref.1, f32[384]{0:T(512)} %bias_ref.1, f32[384]{0:T(512)} %gain_ref.1, bf16[4,2,80,384]{3,2,1,0:T(8,128)(2,1)} %feats_hbm.1, bf16[3,3,1152,384]{3,2,1,0:T(8,128)(2,1)} %bitcast.3, ...), custom_call_target="tpu_custom_call" | custom-call | flops 16000000000 | bytes 12000000 | tf_op jit(solution)/shard_map/pallas_call | solution.py:412
  63.5 2.0 %shard_map.114 = (bf16[4,160,384]{2,1,0:T(8,128)(2,1)}, bf16[4,160,384]{2,1,0:T(8,128)(2,1)}) custom-call(bf16[4,160,384]{2,1,0:T(8,128)(2,1)} %get-tuple-element.6.resid_ref, bf16[4,160,384]{2,1,0:T(8,128)(2,1)} %get-tuple-element.7.mixed_ref), custom_call_target="tpu_custom_call" | custom-call | tf_op jit(solution)/shard_map/pallas_call | solution.py:444

commit v6 on v5

--- a/solution.py
+++ b/solution.py
@@ -325,16 +325,24 @@
         landed(0, 4 + b)
     for tile in tiles:
         attend(0, tile)
-    for group, from_left, from_right in ((1, 0, 2), (2, 1, 3)):
+    def relay(group, from_left, from_right):
         for place, forward, device in ((0, from_left, right), (3, from_right, left), (1, None, None), (2, None, None)):
             landed(group, place)
             if forward is not None:
                 push((group, place), (3, forward), device)
             push((group, place), (group, 4 + place), sibling)
-        for place in range(4):
-            landed(group, 4 + place)
-        for tile in tiles:
-            attend(group, tile)
+
+    relay(1, 0, 2)
+    for place in range(4):
+        landed(1, 4 + place)
+    attend(1, 0)
+    relay(2, 1, 3)
+    for tile in tiles[1:]:
+        attend(1, tile)
+    for place in range(4):
+        landed(2, 4 + place)
+    for tile in tiles:
+        attend(2, tile)
     for b in (0, 2, 1, 3):
         landed(3, b)
         push((3, b), (3, 4 + b), sibling)

time: 65.8 us -> 65.8 us (level)
  the two profiles are of different devices: /device:TPU:41 before, /device:TPU:14 now
where the time goes in v6:
time: 65.8 us; the launch traced here: 65.7 us
  Pallas kernels  64.9 us (99%)
  between operations  0.8 us (1%)
    pallas_call x1, Pallas kernels, local(): pl.pallas_call(block_kernel, out_shape=(half, half), in_specs=[smem] + [v...  62.9 us
    pallas_call x1, Pallas kernels, local(): pl.pallas_call(finish_kernel, out_shape=(half, half), in_specs=[hbm, hbm]...  2 us

profile of v6, /device:TPU:14, one launch (start us, length us, event | category | flops | bytes accessed | tf_op | source)
XLA Modules:
  0.0 65.7 jit_solution(5425459021551222536)
XLA Ops:
  0.6 62.9 %shard_map.113 = (bf16[4,160,384]{2,1,0:T(8,128)(2,1)}, bf16[4,160,384]{2,1,0:T(8,128)(2,1)}) custom-call(s32[3]{0:T(128)} %clip_ref.1, f32[384]{0:T(512)} %norm_gain_ref.1, f32[384]{0:T(512)} %bias_ref.1, f32[384]{0:T(512)} %gain_ref.1, bf16[4,2,80,384]{3,2,1,0:T(8,128)(2,1)} %feats_hbm.1, bf16[3,3,1152,384]{3,2,1,0:T(8,128)(2,1)} %bitcast.3, ...), custom_call_target="tpu_custom_call" | custom-call | flops 16000000000 | bytes 12000000 | tf_op jit(solution)/shard_map/pallas_call | solution.py:420
  63.5 2.0 %shard_map.114 = (bf16[4,160,384]{2,1,0:T(8,128)(2,1)}, bf16[4,160,384]{2,1,0:T(8,128)(2,1)}) custom-call(bf16[4,160,384]{2,1,0:T(8,128)(2,1)} %get-tuple-element.6.resid_ref, bf16[4,160,384]{2,1,0:T(8,128)(2,1)} %get-tuple-element.7.mixed_ref), custom_call_target="tpu_custom_call" | custom-call | tf_op jit(solution)/shard_map/pallas_call | solution.py:452
